TPU v7x, 128 devices: a whole 4x4x4 slice. The times are simulated.
128 devices in a mesh: row: 8 (over y, z_hi), col: 16 (over x, z_lo, core).
Axes of the slice: x: 4, y: 4, z: 4 (z_hi: 2, z_lo: 2; z = z_hi * 2 + z_lo), core: 2. Of those that a mesh axis runs over, the one named last changes fastest.
Arguments:
- tokens: bfloat16 [16448, 1024], P('row', 'col'), may hold values from -6 to 6
- qkv_weight: bfloat16 [1024, 3072], P('col', 'row'), may hold values from -2 to 2
- persistent: bfloat16 [16, 2, 1024], P(None, None, 'row'), may hold values from -6 to 6
- cache_pages: bfloat16 [1024, 256, 2, 1024], P('col', None, None, 'row'), may hold values from -48 to 48
- page_table: int32 [64, 16], P('col'), may hold values from 0 to 63, as said below
- cache_len: int32 [64], P('col'), may hold values from 1 to 4096, as said below
- destination: int32 [16], P('col'), may hold values from 0 to 15, each once
- memory_in: float32 [16, 8, 128, 128], P('col', 'row'), may hold values from -6 to 6
- momentum_in: float32 [16, 8, 128, 128], P('col', 'row'), may hold values from -3 to 3
- forget_rate: float32 [16, 8, 16], P('col', 'row'), may hold values from 0.02 to 0.5
- keep_rate: float32 [16, 8, 16], P('col', 'row'), may hold values from 0.3 to 0.95
- learn_rate: float32 [16, 8, 16], P('col', 'row'), may hold values from 0.05 to 1
- decode_memory: float32 [64, 8, 128, 128], P('col', 'row'), may hold values from -6 to 6
Outputs:
- heads_out: bfloat16 [16448, 1024], P('col', 'row')
- memory_out: float32 [16, 8, 128, 128], P('col', 'row')
- momentum_out: float32 [16, 8, 128, 128], P('col', 'row')
Inputs may be any that keep to these rules, and one draw needn't show every extreme that they name: `page_table`: the 4 decode requests of one index of col together name every page of that index's pool once. `cache_len`: some request has exactly 4096. `destination`: each request block once.
All inputs are finite; a program needn't handle non-finite values.
Results may differ from a plain program's by a relative error of at most 0.012.
The roundings to bfloat16 on the way count: a program that leaves them out, or rounds other values in their place, can miss the bound.
Values may be sent and summed in bfloat16 or wider, within the bound.
No kernel may reach another device: no remote copies, remote signals or barrier semaphores. Data moves between devices by JAX's collectives and lax.ppermute only.
A program may use at most 128 MiB of HBM per device.

v0:
```python
import jax
import jax.numpy as jnp
from jax import lax
from jax.sharding import PartitionSpec as P

HD = 128
PERS = 16
MCH = 64
PCH = 1024
DEC_DEV = 4
CACHE = 4096
epsilon = 1e-06
highest = lax.Precision.HIGHEST


def unit_rows(values):
    return values / jnp.sqrt(jnp.sum(values * values, axis=-1, keepdims=True) + epsilon)


def memory_spans(
    query_unit, key_unit, value_rows, memory, momentum, forget_rate, keep_rate, learn_rate
):

    def advance(carry, inputs):
        memory_now, momentum_now = carry
        query_now, key_now, value_now, forget_now, keep_now, learn_now = inputs
        readout = jnp.dot(query_now, memory_now, precision=highest)
        errors = jnp.dot(key_now, memory_now, precision=highest) - value_now
        gradient = jnp.dot(key_now.T, errors, precision=highest) * (2.0 / MCH)
        momentum_now = keep_now * momentum_now - learn_now * gradient
        memory_now = (1.0 - forget_now) * memory_now + momentum_now
        return ((memory_now, momentum_now), readout)

    (memory, momentum), readouts = lax.scan(
        advance,
        (memory, momentum),
        (query_unit, key_unit, value_rows, forget_rate, keep_rate, learn_rate),
    )
    return (readouts, memory, momentum)


def window_attention(query_rows, key_rows, value_rows, persist_key, persist_value):
    scale_factor = query_rows.shape[-1] ** (-0.5)
    inner_score = (
        jnp.einsum("nqd,nkd->nqk", query_rows, key_rows, preferred_element_type=jnp.float32)
        * scale_factor
    )
    length_q = query_rows.shape[1]
    causal = jnp.arange(length_q)[:, None] >= jnp.arange(length_q)[None, :]
    inner_score = jnp.where(causal[None], inner_score, -jnp.inf)
    outer_score = (
        jnp.einsum("nqd,pd->nqp", query_rows, persist_key, preferred_element_type=jnp.float32)
        * scale_factor
    )
    highest_score = jnp.maximum(jnp.max(inner_score, axis=-1), jnp.max(outer_score, axis=-1))[
        ..., None
    ]
    inner_exp = jnp.exp(inner_score - highest_score)
    outer_exp = jnp.exp(outer_score - highest_score)
    totals = jnp.sum(inner_exp, axis=-1, keepdims=True) + jnp.sum(outer_exp, axis=-1, keepdims=True)
    inner_weight = (inner_exp / totals).astype(jnp.bfloat16)
    outer_weight = (outer_exp / totals).astype(jnp.bfloat16)
    attended = jnp.einsum(
        "nqk,nkd->nqd", inner_weight, value_rows, preferred_element_type=jnp.float32
    )
    return attended + jnp.einsum(
        "nqp,pd->nqd", outer_weight, persist_value, preferred_element_type=jnp.float32
    )


def prefill_head(
    token_block, persist_key, persist_value, memory, momentum, forget_rate, keep_rate, learn_rate
):
    spans = token_block.shape[0] // MCH
    query_rows = token_block[:, 0].reshape(spans, MCH, -1)
    key_rows = token_block[:, 1].reshape(spans, MCH, -1)
    value_rows = token_block[:, 2].reshape(spans, MCH, -1)
    readouts, memory, momentum = memory_spans(
        unit_rows(query_rows.astype(jnp.float32)),
        unit_rows(key_rows.astype(jnp.float32)),
        value_rows.astype(jnp.float32),
        memory,
        momentum,
        forget_rate,
        keep_rate,
        learn_rate,
    )
    attended = window_attention(query_rows, key_rows, value_rows, persist_key, persist_value)
    return (
        (attended + readouts).reshape(-1, token_block.shape[-1]).astype(jnp.bfloat16),
        memory,
        momentum,
    )


def decode_block(row_block, cache_block, persist_key, persist_value, memory_now, length_now):
    scale_factor = row_block.shape[-1] ** (-0.5)
    query_row = row_block[:, 0]
    key_row = row_block[:, 1]
    value_row = row_block[:, 2]
    cache_score = (
        jnp.einsum("chd,hd->hc", cache_block[:, 0], query_row, preferred_element_type=jnp.float32)
        * scale_factor
    )
    live_mask = jnp.arange(cache_block.shape[0]) < length_now
    cache_score = jnp.where(live_mask[None, :], cache_score, -jnp.inf)
    own_score = (
        jnp.sum(query_row.astype(jnp.float32) * key_row.astype(jnp.float32), axis=-1) * scale_factor
    )
    persist_score = (
        jnp.einsum("phd,hd->hp", persist_key, query_row, preferred_element_type=jnp.float32)
        * scale_factor
    )
    highest_score = jnp.maximum(
        jnp.maximum(jnp.max(cache_score, axis=-1), own_score), jnp.max(persist_score, axis=-1)
    )
    cache_exp = jnp.exp(cache_score - highest_score[:, None])
    own_exp = jnp.exp(own_score - highest_score)
    persist_exp = jnp.exp(persist_score - highest_score[:, None])
    totals = jnp.sum(cache_exp, axis=-1) + own_exp + jnp.sum(persist_exp, axis=-1)
    cache_weight = (cache_exp / totals[:, None]).astype(jnp.bfloat16)
    own_weight = (own_exp / totals).astype(jnp.bfloat16)
    persist_weight = (persist_exp / totals[:, None]).astype(jnp.bfloat16)
    attended = jnp.einsum(
        "hc,chd->hd", cache_weight, cache_block[:, 1], preferred_element_type=jnp.float32
    )
    attended = attended + own_weight.astype(jnp.float32)[:, None] * value_row.astype(jnp.float32)
    attended = attended + jnp.einsum(
        "hp,phd->hd", persist_weight, persist_value, preferred_element_type=jnp.float32
    )
    readout = jnp.einsum(
        "hd,hde->he", unit_rows(query_row.astype(jnp.float32)), memory_now, precision=highest
    )
    return (attended + readout).astype(jnp.bfloat16)


def shards(
    tokens,
    qkv_weight,
    persistent,
    cache_pages,
    page_table,
    cache_len,
    destination,
    memory_in,
    momentum_in,
    forget_rate,
    keep_rate,
    learn_rate,
    decode_memory,
):
    block_rows = PCH + DEC_DEV
    heads_dev = qkv_weight.shape[1] // (3 * HD)
    gathered = lax.all_gather(tokens, "row", axis=0, tiled=True)
    projected = lax.psum_scatter(
        jnp.dot(gathered, qkv_weight, preferred_element_type=jnp.float32),
        "col",
        scatter_dimension=0,
        tiled=True,
    )
    projected = projected.astype(jnp.bfloat16).reshape(block_rows, heads_dev, 3, HD)
    slot_count = lax.axis_size("col")
    target = (jnp.arange(slot_count, dtype=jnp.int32) == destination[0]).astype(jnp.float32)
    states = jnp.stack([memory_in[0], momentum_in[0]], axis=0)
    outgoing = target[:, None, None, None, None] * states[None]
    arrived = jnp.sum(
        lax.all_to_all(outgoing, "col", split_axis=0, concat_axis=0, tiled=True), axis=0
    )
    persist = persistent.reshape(PERS, 2, heads_dev, HD)
    out_rows, memory_next, momentum_next = prefill_head(
        projected[:PCH, 0],
        persist[:, 0, 0],
        persist[:, 1, 0],
        arrived[0, 0],
        arrived[1, 0],
        forget_rate[0, 0],
        keep_rate[0, 0],
        learn_rate[0, 0],
    )
    prefill_list = [out_rows]
    memory_list = [memory_next]
    momentum_list = [momentum_next]
    caches = cache_pages[page_table.reshape(-1)].reshape(DEC_DEV, CACHE, 2, heads_dev, HD)
    decode_map = jax.vmap(decode_block, in_axes=(0, 0, None, None, 0, 0))
    decode_out = decode_map(
        projected[PCH:], caches, persist[:, 0], persist[:, 1], decode_memory, cache_len
    )
    prefill_out = jnp.stack(prefill_list, axis=1)
    heads_out = jnp.concatenate([prefill_out, decode_out], axis=0).reshape(
        block_rows, heads_dev * HD
    )
    return (heads_out, jnp.stack(memory_list, axis=0)[None], jnp.stack(momentum_list, axis=0)[None])


def solution(mesh):
    placed = (
        P("row", "col"),
        P("col", "row"),
        P(None, None, "row"),
        P("col", None, None, "row"),
        P("col", None),
        P("col"),
        P("col"),
        P("col", "row", None, None),
        P("col", "row", None, None),
        P("col", "row", None),
        P("col", "row", None),
        P("col", "row", None),
        P("col", "row", None, None),
    )
    return jax.shard_map(
        shards,
        mesh=mesh,
        in_specs=placed,
        out_specs=(P("col", "row"), P("col", "row", None, None), P("col", "row", None, None)),
        check_vma=False,
    )
```

profile of v0, /device:TPU:1, one launch (start us, length us, event | category | flops | bytes accessed | tf_op | source)
XLA Modules:
  0.0 477.1 jit_solution(6140073066499957147)
XLA Ops:
  9.5 1.6 broadcast_multiply_fusion
  11.1 7.2 %all-to-all-start = ((f32[16,2,1,128,128]{4,3,2,1,0:T(8,128)}), f32[16,2,1,128,128]{4,3,2,1,0:T(8,128)S(1)}, u32[]{:S(2)}, u32[]{:S(2)}) async-start(f32[16,2,1,128,128]{4,3,2,1,0:T(8,128)} %broadcast_multiply_fusion), calls=%async_computation | async-start | bytes 4194304 | tf_op jit(solution)/shard_map/all_to_all | solution.py:167
  18.4 22.1 %gather_fusion = bf16[64,256,2,128]{3,2,1,0:T(2,128)(2,1)} fusion(bf16[64,256,2,128]{3,2,1,0:T(2,128)(2,1)} %param.18, s32[1024]{0:T(1024)S(1)} %pad_clamp_fusion), kind=kCustom, calls=%fused_computation | custom fusion | bytes 16777472 | tf_op jit(solution)/shard_map/gather | solution.py:183
  40.5 8.8 %copy.43 = bf16[64,256,2,128]{3,1,0,2:T(8,128)(2,1)} copy(bf16[64,256,2,128]{3,2,1,0:T(2,128)(2,1)} %gather_fusion) | data formatting | bytes 16777216 | tf_op jit(solution)/shard_map/gather | solution.py:183
  50.7 34.3 %all-gather.3.cloned.1.call-done = bf16[8,2056,64]{1,2,0:T(8,128)(2,1)} async-done(((bf16[1,2056,64]{1,2,0:T(8,128)(2,1)}), bf16[8,2056,64]{1,2,0:T(8,128)(2,1)}) %all-gather.3.cloned.1.call-update) | async-done | bytes 2105360 | tf_op jit(solution)/shard_map/all_gather | solution.py:154
  85.0 2.9 copy.36
  87.9 3.0 reshape.345
  90.9 13.4 %fusion.56 = f32[16448,384]{1,0:T(8,128)} fusion(bf16[16448,64]{0,1:T(8,128)(2,1)} %reshape.345, bf16[64,384]{1,0:T(8,128)(2,1)S(1)} %copy-done.4), kind=kOutput, calls=%fused_computation.104 | convolution fusion | flops 808452096 | bytes 27418624 | tf_op jit(solution)/shard_map/dot_general | solution.py:156
  104.3 271.0 %fusion = f32[1040,384]{1,0:T(8,128)S(1)} fusion(f32[16448,384]{1,0:T(8,128)} %fusion.56), kind=kCustom, calls=%all-reduce-scatter | all-reduce-scatter fusion | flops 6389761 | bytes 26862080
  375.3 4.6 collective-permute-start
  379.9 1.8 collective-permute-done
  381.7 2.1 concatenate.4
  386.8 1.1 fusion.23
  388.5 73.0 %while.14 = (s32[]{:T(128)}, f32[128,128]{1,0:T(8,128)S(1)}, f32[128,128]{1,0:T(8,128)S(1)}, f32[16,64,128]{2,1,0:T(8,128)S(1)}, f32[16]{0:T(128)S(1)}, /*index=...) while((s32[]{:T(128)}, f32[128,128]{1,0:T(8,128)S(1)}, ...), condition=%wide.region_9.10_spmd, body=%wide.region_8.9_spmd.sunk | while | flops 37838852 | bytes 624841 | solution.py:34
  392.1 1.0 multiply_add_fusion.2
  396.7 1.0 multiply_add_fusion.2
  401.2 1.0 multiply_add_fusion.2
  405.8 1.0 multiply_add_fusion.2
  410.3 1.0 multiply_add_fusion.2
  414.9 1.0 multiply_add_fusion.2
  419.5 1.0 multiply_add_fusion.2
  424.0 1.0 multiply_add_fusion.2
  428.6 1.0 multiply_add_fusion.2
  433.2 1.0 multiply_add_fusion.2
  437.7 1.0 multiply_add_fusion.2
  442.3 1.0 multiply_add_fusion.2
  446.8 1.0 multiply_add_fusion.2
  451.4 1.0 multiply_add_fusion.2
  456.0 1.0 multiply_add_fusion.2
  460.5 1.0 multiply_add_fusion.2
  461.6 3.4 fusion.13
  465.8 2.8 fusion.12
  (156 shorter events, 43.8 us)
Async XLA Ops:
  7.2 461.9 %copy-start = (f32[4,1,128,128]{3,2,1,0:T(8,128)S(1)}, f32[4,1,128,128]{3,2,1,0:T(8,128)}, u32[]{:S(2)}) copy-start(f32[4,1,128,128]{3,2,1,0:T(8,128)} %param.27) | copy-start | bytes 786436
  7.2 11.1 %copy-start.5 = (bf16[16,2,128]{2,1,0:T(2,128)(2,1)S(1)}, bf16[16,2,128]{2,1,0:T(2,128)(2,1)}, u32[]{:S(2)}) copy-start(bf16[16,2,128]{2,1,0:T(2,128)(2,1)} %param.17) | copy-start | bytes 24580
  7.2 11.1 %copy-start.6 = (s32[4,16]{1,0:T(4,128)S(1)}, s32[4,16]{1,0:T(4,128)}, u32[]{:S(2)}) copy-start(s32[4,16]{1,0:T(4,128)} %param.19) | copy-start | bytes 772
  7.2 77.8 %all-gather.3.cloned.1.call-start = ((), (), s32[]{:S(2)}) async-start(), calls=%async_computation.1 | async-start | bytes 2506752 | tf_op jit(solution)/shard_map/all_gather | solution.py:154
  11.1 39.5 %all-to-all-start = ((f32[16,2,1,128,128]{4,3,2,1,0:T(8,128)}), f32[16,2,1,128,128]{4,3,2,1,0:T(8,128)S(1)}, u32[]{:S(2)}, u32[]{:S(2)}) async-start(f32[16,2,1,128,128]{4,3,2,1,0:T(8,128)} %broadcast_multiply_fusion), calls=%async_computation | async-start | bytes 4194304 | tf_op jit(solution)/shard_map/all_to_all | solution.py:167
  40.5 8.8 %copy-start.8 = (u32[128]{0:T(128)S(1)}, u32[128]{0:T(128)}, u32[]{:S(2)}) copy-start(u32[128]{0:T(128)} %constant.47) | copy-start | bytes 1540
  50.7 40.2 %copy-start.4 = (bf16[64,384]{1,0:T(8,128)(2,1)S(1)}, bf16[64,384]{1,0:T(8,128)(2,1)}, u32[]{:S(2)}) copy-start(bf16[64,384]{1,0:T(8,128)(2,1)} %param.16) | copy-start | bytes 147460
  375.3 6.4 %collective-permute-start = (bf16[180,384]{1,0:T(8,128)(2,1)S(1)}, bf16[180,384]{1,0:T(8,128)(2,1)}, u32[]{:S(2)}, u32[]{:S(2)}) collective-permute-start(bf16[180,384]{1,0:T(8,128)(2,1)S(1)} %slice.81), channel_id=1, source_target_pairs={{0,1},{1,2},{2,3},{3,4},{4,5},{5,6},{6,7},{7,8},{8,9},{9,10},{10,1... | collective-permute-start | bytes 414728
  385.2 3.3 copy-start.9
  385.2 3.3 copy-start.10
  385.2 3.3 copy-start.11
  388.5 76.5 %copy-start.7 = (s32[4]{0:T(128)S(1)}, s32[4]{0:T(128)}, u32[]{:S(2)}) copy-start(s32[4]{0:T(128)} %param.20) | copy-start | bytes 52
  461.5 7.1 %copy-start.1 = (f32[128,128]{1,0:T(8,128)}, f32[128,128]{1,0:T(8,128)S(1)}, u32[]{:S(2)}) copy-start(f32[128,128]{1,0:T(8,128)S(1)} %get-tuple-element.58) | copy-start | bytes 196612
  461.6 7.1 %copy-start.2 = (f32[128,128]{1,0:T(8,128)}, f32[128,128]{1,0:T(8,128)S(1)}, u32[]{:S(2)}) copy-start(f32[128,128]{1,0:T(8,128)S(1)} %get-tuple-element.59) | copy-start | bytes 196612
  461.6 7.1 %copy-start.3 = (f32[16,64,128]{2,1,0:T(8,128)S(1)}, f32[16,64,128]{2,1,0:T(8,128)}, u32[]{:S(2)}) copy-start(f32[16,64,128]{2,1,0:T(8,128)} %fusion.23) | copy-start | bytes 1572868
Sparse Core Ops, SparseCore 0:
  10.3 74.6 all-gather.2
where the time goes:
time: 478 us; the launch traced here: 477 us
  blocking collectives  271 us (57%)
  local copies, waits for them, and re-layouts  70.9 us (15%)
  matrix products  44.4 us (9%)
  waiting for transfers between devices  36.8 us (8%)
  loops' own time  21.4 us (4%)
  between operations  15.7 us (3%)
  starting transfers between devices  11.8 us (2%)
  other arithmetic  5.13 us (1%)
    unnamed x1, blocking collectives  271 us
    all_gather x1, waiting for transfers between devices, shards(): gathered = lax.all_gather(tokens, 'row', axis=0, tiled=True)  34.3 us
    gather x2, local copies, waits for them, and re-layouts, shards(): cache_pages[page_table.reshape(-1)]  30.9 us
    dynamic_slice x48, local copies, waits for them, and re-layouts, memory_spans(): lax.scan(advance, (memory, momentum), (query_unit, key_unit, value_rows,...  29.6 us
    another operation x1, loops' own time, memory_spans(): lax.scan(advance, (memory, momentum), (query_unit, key_unit, value_rows,...  21.4 us
    dot_general x16, matrix products, advance(): gradient = jnp.dot(key_now.T, errors, precision=highest) * (2.0 / MCH)  16 us
    dot_general x1, matrix products, shards(): jnp.dot(gathered, qkv_weight, preferred_element_type=jnp.float32)  13.4 us
  transfers between devices with their start and end apart: 3, of which 2 were waited for; matrix products, arithmetic and copies ran while one was open for 7% of the time, Pallas kernels for 0%

commit v1 on v0

--- a/solution.py
+++ b/solution.py
@@ -151,7 +151,8 @@
 ):
     block_rows = PCH + DEC_DEV
     heads_dev = qkv_weight.shape[1] // (3 * HD)
-    gathered = lax.all_gather(tokens, "row", axis=0, tiled=True)
+    sent = jnp.stack([tokens] * lax.axis_size("row"))
+    gathered = jnp.concatenate(lax.all_to_all(sent, "row", 0, 0), axis=0)
     projected = lax.psum_scatter(
         jnp.dot(gathered, qkv_weight, preferred_element_type=jnp.float32),
         "col",

time: 478 us -> 438 us (0.916)
  waiting for transfers between devices: 36.8 us -> 0.1 us
  between operations: 15.7 us -> 2.37 us
  starting transfers between devices: 11.8 us -> 18.6 us
    all_gather x1 -> x0, waiting for transfers between devices: 34.3 us -> none  [shards(): gathered = lax.all_gather(tokens, 'row', axis=0, tiled=True)]
    all_to_all x0 -> x1, starting transfers between devices: none -> 8.33 us  [shards(): gathered = jnp.concatenate(lax.all_to_all(sent, 'row', 0, 0), axis=0)]
  transfers between devices with their start and end apart: 3 -> 3, of which waited for: 2 -> 1; matrix products, arithmetic and copies ran while one was open for 7% -> 74% of each run, Pallas kernels for 0% -> 0%
where the time goes in v1:
time: 438 us; the launch traced here: 437 us
  blocking collectives  273 us (62%)
  local copies, waits for them, and re-layouts  74 us (17%)
  matrix products  41.1 us (9%)
  loops' own time  21.4 us (5%)
  starting transfers between devices  18.6 us (4%)
  other arithmetic  5.86 us (1%)
    unnamed x1, blocking collectives  273 us
    gather x2, local copies, waits for them, and re-layouts, shards(): cache_pages[page_table.reshape(-1)]  31 us
    dynamic_slice x48, local copies, waits for them, and re-layouts, memory_spans(): lax.scan(advance, (memory, momentum), (query_unit, key_unit, value_rows,...  29.6 us
    another operation x1, loops' own time, memory_spans(): lax.scan(advance, (memory, momentum), (query_unit, key_unit, value_rows,...  21.4 us
    dot_general x16, matrix products, advance(): gradient = jnp.dot(key_now.T, errors, precision=highest) * (2.0 / MCH)  16 us
    dot_general x1, matrix products, shards(): jnp.dot(gathered, qkv_weight, preferred_element_type=jnp.float32)  10.2 us
  transfers between devices with their start and end apart: 3, of which 1 were waited for; matrix products, arithmetic and copies ran while one was open for 74% of the time, Pallas kernels for 0%

profile of v1, /device:TPU:1, one launch (start us, length us, event | category | flops | bytes accessed | tf_op | source)
XLA Modules:
  0.0 436.9 jit_solution(920388106208024397)
XLA Ops:
  0.7 2.7 stack.4
  3.3 8.3 %all-to-all-start = ((bf16[8,2056,64]{1,2,0:T(8,128)(2,1)}), bf16[8,2056,64]{1,2,0:T(8,128)(2,1)S(1)}, u32[]{:S(2)}, u32[]{:S(2)}) async-start(bf16[8,2056,64]{1,2,0:T(8,128)(2,1)} %stack.4), calls=%async_computation | async-start | bytes 4456448 | tf_op jit(solution)/shard_map/all_to_all | solution.py:155
  12.4 22.1 %gather_fusion = bf16[64,256,2,128]{3,2,1,0:T(2,128)(2,1)} fusion(bf16[64,256,2,128]{3,2,1,0:T(2,128)(2,1)} %param.18, s32[1024]{0:T(1024)S(1)} %pad_clamp_fusion), kind=kCustom, calls=%fused_computation | custom fusion | bytes 16777472 | tf_op jit(solution)/shard_map/gather | solution.py:184
  34.6 8.9 %copy.52 = bf16[64,256,2,128]{3,1,0,2:T(8,128)(2,1)} copy(bf16[64,256,2,128]{3,2,1,0:T(2,128)(2,1)} %gather_fusion) | data formatting | bytes 16777216 | tf_op jit(solution)/shard_map/gather | solution.py:184
  44.7 1.6 broadcast_multiply_fusion
  46.3 5.7 %all-to-all-start.1 = ((f32[16,2,1,128,128]{4,3,2,1,0:T(8,128)}), f32[16,2,1,128,128]{4,3,2,1,0:T(8,128)}, u32[]{:S(2)}, u32[]{:S(2)}) async-start(f32[16,2,1,128,128]{4,3,2,1,0:T(8,128)} %broadcast_multiply_fusion), calls=%async_computation.1 | async-start | bytes 4194304 | tf_op jit(solution)/shard_map/all_to_all | solution.py:168
  52.1 2.6 copy.45
  54.7 3.6 reshape.331
  58.4 10.2 %fusion.56 = f32[16448,384]{1,0:T(8,128)} fusion(bf16[16448,64]{0,1:T(8,128)(2,1)S(1)} %reshape.331, bf16[64,384]{1,0:T(8,128)(2,1)S(1)} %copy-done.6), kind=kOutput, calls=%fused_computation.104 | convolution fusion | flops 808452096 | bytes 27418624 | tf_op jit(solution)/shard_map/dot_general | solution.py:157
  68.5 273.4 %fusion = f32[1040,384]{1,0:T(8,128)S(1)} fusion(f32[16448,384]{1,0:T(8,128)} %fusion.56), kind=kCustom, calls=%all-reduce-scatter | all-reduce-scatter fusion | flops 6389761 | bytes 26862080
  342.0 4.6 %collective-permute-start = (bf16[180,384]{1,0:T(8,128)(2,1)S(1)}, bf16[180,384]{1,0:T(8,128)(2,1)}, u32[]{:S(2)}, u32[]{:S(2)}) collective-permute-start(bf16[180,384]{1,0:T(8,128)(2,1)S(1)} %slice.81), channel_id=1, source_target_pairs={{0,1},{1,2},{2,3},{3,4},{4,5},{5,6},{6,7},{7,8},{8,9},{9,10},{10,1... | collective-permute-start | bytes 414728
  346.6 1.7 reduce_sum.83
  348.4 2.1 concatenate.4
  353.5 1.1 fusion.23
  355.2 73.0 %while.14 = (s32[]{:T(128)}, f32[128,128]{1,0:T(8,128)S(1)}, f32[128,128]{1,0:T(8,128)S(1)}, f32[16,64,128]{2,1,0:T(8,128)S(1)}, f32[16]{0:T(128)S(1)}, /*index=...) while((s32[]{:T(128)}, f32[128,128]{1,0:T(8,128)S(1)}, ...), condition=%wide.region_9.10_spmd, body=%wide.region_8.9_spmd.sunk | while | flops 37838852 | bytes 624841 | solution.py:34
  358.8 1.0 multiply_add_fusion.2
  363.3 1.0 multiply_add_fusion.2
  367.9 1.0 multiply_add_fusion.2
  372.4 1.0 multiply_add_fusion.2
  377.0 1.0 multiply_add_fusion.2
  381.6 1.0 multiply_add_fusion.2
  386.1 1.0 multiply_add_fusion.2
  390.7 1.0 multiply_add_fusion.2
  395.3 1.0 multiply_add_fusion.2
  399.8 1.0 multiply_add_fusion.2
  404.4 1.0 multiply_add_fusion.2
  408.9 1.0 multiply_add_fusion.2
  413.5 1.0 multiply_add_fusion.2
  418.1 1.0 multiply_add_fusion.2
  422.6 1.0 multiply_add_fusion.2
  428.2 3.4 fusion.13
  432.5 2.8 fusion.12
  (160 shorter events, 43.2 us)
Async XLA Ops:
  0.6 435.1 %copy-start = (f32[4,1,128,128]{3,2,1,0:T(8,128)S(1)}, f32[4,1,128,128]{3,2,1,0:T(8,128)}, u32[]{:S(2)}) copy-start(f32[4,1,128,128]{3,2,1,0:T(8,128)} %param.27) | copy-start | bytes 786436
  0.6 11.0 %copy-start.7 = (bf16[16,2,128]{2,1,0:T(2,128)(2,1)S(1)}, bf16[16,2,128]{2,1,0:T(2,128)(2,1)}, u32[]{:S(2)}) copy-start(bf16[16,2,128]{2,1,0:T(2,128)(2,1)} %param.17) | copy-start | bytes 24580
  0.7 11.7 %copy-start.8 = (s32[4,16]{1,0:T(4,128)S(1)}, s32[4,16]{1,0:T(4,128)}, u32[]{:S(2)}) copy-start(s32[4,16]{1,0:T(4,128)} %param.19) | copy-start | bytes 772
  3.3 43.0 %all-to-all-start = ((bf16[8,2056,64]{1,2,0:T(8,128)(2,1)}), bf16[8,2056,64]{1,2,0:T(8,128)(2,1)S(1)}, u32[]{:S(2)}, u32[]{:S(2)}) async-start(bf16[8,2056,64]{1,2,0:T(8,128)(2,1)} %stack.4), calls=%async_computation | async-start | bytes 4456448 | tf_op jit(solution)/shard_map/all_to_all | solution.py:155
  34.6 8.9 %copy-start.10 = (u32[128]{0:T(128)S(1)}, u32[128]{0:T(128)}, u32[]{:S(2)}) copy-start(u32[128]{0:T(128)} %constant.47) | copy-start | bytes 1540
  34.6 10.1 %copy-start.4 = (f32[1,1,128,128]{3,2,1,0:T(8,128)S(1)}, f32[1,1,128,128]{3,2,1,0:T(8,128)}, u32[]{:S(2)}) copy-start(f32[1,1,128,128]{3,2,1,0:T(8,128)} %param.23) | copy-start | bytes 196612
  34.6 10.1 %copy-start.5 = (f32[1,1,128,128]{3,2,1,0:T(8,128)S(1)}, f32[1,1,128,128]{3,2,1,0:T(8,128)}, u32[]{:S(2)}) copy-start(f32[1,1,128,128]{3,2,1,0:T(8,128)} %param.22) | copy-start | bytes 196612
  46.3 300.2 %all-to-all-start.1 = ((f32[16,2,1,128,128]{4,3,2,1,0:T(8,128)}), f32[16,2,1,128,128]{4,3,2,1,0:T(8,128)}, u32[]{:S(2)}, u32[]{:S(2)}) async-start(f32[16,2,1,128,128]{4,3,2,1,0:T(8,128)} %broadcast_multiply_fusion), calls=%async_computation.1 | async-start | bytes 4194304 | tf_op jit(solution)/shard_map/all_to_all | solution.py:168
  52.1 6.3 %copy-start.6 = (bf16[64,384]{1,0:T(8,128)(2,1)S(1)}, bf16[64,384]{1,0:T(8,128)(2,1)}, u32[]{:S(2)}) copy-start(bf16[64,384]{1,0:T(8,128)(2,1)} %param.16) | copy-start | bytes 147460
  342.0 6.4 %collective-permute-start = (bf16[180,384]{1,0:T(8,128)(2,1)S(1)}, bf16[180,384]{1,0:T(8,128)(2,1)}, u32[]{:S(2)}, u32[]{:S(2)}) collective-permute-start(bf16[180,384]{1,0:T(8,128)(2,1)S(1)} %slice.81), channel_id=1, source_target_pairs={{0,1},{1,2},{2,3},{3,4},{4,5},{5,6},{6,7},{7,8},{8,9},{9,10},{10,1... | collective-permute-start | bytes 414728
  351.8 3.3 copy-start.11
  351.8 3.3 copy-start.12
  351.8 3.3 copy-start.13
  355.2 76.5 %copy-start.9 = (s32[4]{0:T(128)S(1)}, s32[4]{0:T(128)}, u32[]{:S(2)}) copy-start(s32[4]{0:T(128)} %param.20) | copy-start | bytes 52
  428.2 7.1 %copy-start.1 = (f32[128,128]{1,0:T(8,128)}, f32[128,128]{1,0:T(8,128)S(1)}, u32[]{:S(2)}) copy-start(f32[128,128]{1,0:T(8,128)S(1)} %get-tuple-element.58) | copy-start | bytes 196612
  428.2 7.1 %copy-start.2 = (f32[128,128]{1,0:T(8,128)}, f32[128,128]{1,0:T(8,128)S(1)}, u32[]{:S(2)}) copy-start(f32[128,128]{1,0:T(8,128)S(1)} %get-tuple-element.59) | copy-start | bytes 196612
  428.2 7.1 %copy-start.3 = (f32[16,64,128]{2,1,0:T(8,128)S(1)}, f32[16,64,128]{2,1,0:T(8,128)}, u32[]{:S(2)}) copy-start(f32[16,64,128]{2,1,0:T(8,128)} %fusion.23) | copy-start | bytes 1572868
